TPU v7x, 32 devices: a whole 2x2x4 slice. The times are simulated.
32 devices in a mesh: dp: 4 (over y, x), seq: 8 (over z, core).
Axes of the slice: x: 2, y: 2, z: 4, core: 2. Of those that a mesh axis runs over, the one named last changes fastest.
Arguments:
- tokens: bfloat16 [10240, 2048], P(('dp', 'seq')), may hold values from -6 to 6
- lengths: int32 [4, 2], P('dp'), may hold values from 1 to 2048, 2560 in all within a row
- attention_gain: bfloat16 [2048], P('seq'), may hold values from 0.5 to 1.5
- query_weight: bfloat16 [2048, 2048], P('seq'), may hold values from -0.1875 to 0.1875
- key_weight: bfloat16 [2048, 256], P('seq'), may hold values from -0.1875 to 0.1875
- value_weight: bfloat16 [2048, 256], P('seq'), may hold values from -0.125 to 0.125
- output_weight: bfloat16 [2048, 2048], P('seq'), may hold values from -0.375 to 0.375
- feedforward_gain: bfloat16 [2048], P('seq'), may hold values from 0.5 to 1.5
- gate_weight: bfloat16 [2048, 5632], P('seq'), may hold values from -0.125 to 0.125
- up_weight: bfloat16 [2048, 5632], P('seq'), may hold values from -0.125 to 0.125
- down_weight: bfloat16 [5632, 2048], P('seq'), may hold values from -0.078125 to 0.078125
- cotangent: bfloat16 [10240, 2048], P(('dp', 'seq')), may hold values from -6 to 6
Outputs:
- layer_output: bfloat16 [10240, 2048], P(('dp', 'seq'))
- token_gradient: float32 [10240, 2048], P(('dp', 'seq'))
- attention_gain_gradient: float32 [2048], P('seq')
- query_gradient: float32 [2048, 2048], P('seq')
- key_gradient: float32 [2048, 256], P('seq')
- value_gradient: float32 [2048, 256], P('seq')
- output_gradient: float32 [2048, 2048], P('seq')
- feedforward_gain_gradient: float32 [2048], P('seq')
- gate_gradient: float32 [2048, 5632], P('seq')
- up_gradient: float32 [2048, 5632], P('seq')
- down_gradient: float32 [5632, 2048], P('seq')
Inputs may be any that keep to these rules, and one draw needn't show every extreme that they name: Each row lists the lengths of the 2 sequences packed in order into one data group's 2560 tokens; a row sums to 2560 and its longest length is at most 2048.
All inputs are finite; a program needn't handle non-finite values.
Results may differ from a plain program's by a relative error of at most 0.022.
Values may be sent and summed in bfloat16 or wider, within the bound.
No kernel may reach another device: no remote copies, remote signals or barrier semaphores. Data moves between devices by JAX's collectives and lax.ppermute only.
A program may use at most 384 MiB of HBM per device.

v0:
```python
import jax
import jax.numpy as jnp
from jax import lax
from jax.sharding import PartitionSpec as P

D = 2048
HEADS = 32
HEAD_DIM = 64
KV_HEADS = 4
QBLOCK = 512
WINDOW = 2560


EPS = 1e-05
ROPE_BASE = 10000.0
NEG = -1e30


def layout(lengths_row, count):
    ends = jnp.cumsum(lengths_row)
    starts = ends - lengths_row
    index = jnp.arange(count, dtype=jnp.int32)
    segment = jnp.sum((index[:, None] >= ends[None, :]).astype(jnp.int32), axis=1)
    owner = segment[:, None] == jnp.arange(lengths_row.shape[0], dtype=jnp.int32)[None, :]
    first = jnp.sum(jnp.where(owner, starts[None, :], 0), axis=1)
    return (segment, index - first)


def angles(position):
    half = HEAD_DIM // 2
    inverse = ROPE_BASE ** (-jnp.arange(half, dtype=jnp.float32) * 2.0 / HEAD_DIM)
    theta = position.astype(jnp.float32)[:, None] * inverse[None, :]
    return (jnp.cos(theta)[:, None, :], jnp.sin(theta)[:, None, :])


def rotate(values, cos_t, sin_t, sign):
    half = values.shape[-1] // 2
    first = values[..., :half]
    second = values[..., half:]
    return jnp.concatenate(
        [first * cos_t - sign * second * sin_t, second * cos_t + sign * first * sin_t], axis=-1
    )


def dot_plain(left, right):
    return jnp.dot(left, right, preferred_element_type=jnp.float32)


def dot_left(left, right):
    return lax.dot_general(
        left, right, (((0,), (0,)), ((), ())), preferred_element_type=jnp.float32
    )


def dot_right(left, right):
    return lax.dot_general(
        left, right, (((1,), (1,)), ((), ())), preferred_element_type=jnp.float32
    )


def norm_back(upstream, inputs, scale):
    inner = jnp.mean(upstream * inputs, axis=1, keepdims=True)
    return scale * upstream - inputs * scale * scale * scale * inner


def block_scores(queries, keys, segment, position, number):
    row = number * QBLOCK
    first = jnp.maximum(row + QBLOCK - WINDOW, 0)
    q_rows = lax.dynamic_slice_in_dim(queries, row, QBLOCK, 0)
    k_rows = lax.dynamic_slice_in_dim(keys, first, WINDOW, 0)
    seg_q = lax.dynamic_slice_in_dim(segment, row, QBLOCK, 0)
    pos_q = lax.dynamic_slice_in_dim(position, row, QBLOCK, 0)
    seg_k = lax.dynamic_slice_in_dim(segment, first, WINDOW, 0)
    pos_k = lax.dynamic_slice_in_dim(position, first, WINDOW, 0)
    allowed = (seg_q[:, None] == seg_k[None, :]) & (pos_k[None, :] <= pos_q[:, None])
    raw = jnp.einsum(
        "qhd,khd->hqk", q_rows, k_rows, preferred_element_type=jnp.float32
    ) * HEAD_DIM ** (-0.5)
    return (row, first, q_rows, k_rows, allowed, raw)


def attend(queries, keys, values, segment, position):
    blocks = queries.shape[0] // QBLOCK

    def one_block(number):
        row, first, q_rows, k_rows, allowed, raw = block_scores(
            queries, keys, segment, position, number
        )
        v_rows = lax.dynamic_slice_in_dim(values, first, WINDOW, 0)
        scores = jnp.where(allowed[None], raw, NEG)
        top = jnp.max(scores, axis=-1, keepdims=True)
        expo = jnp.exp(scores - top)
        total = jnp.sum(expo, axis=-1, keepdims=True)
        weights = (expo / total).astype(jnp.bfloat16)
        out = jnp.einsum("hqk,khd->qhd", weights, v_rows, preferred_element_type=jnp.float32)
        return (out.astype(jnp.bfloat16), (top + jnp.log(total))[..., 0])

    out, logsum = lax.map(one_block, jnp.arange(blocks, dtype=jnp.int32))
    return (out.reshape(queries.shape), logsum)


def attend_back(queries, keys, values, upstream, logsum, segment, position):
    blocks = queries.shape[0] // QBLOCK
    scale = HEAD_DIM ** (-0.5)

    def one_block(carry, number):
        key_acc, value_acc = carry
        row, first, q_rows, k_rows, allowed, raw = block_scores(
            queries, keys, segment, position, number
        )
        v_rows = lax.dynamic_slice_in_dim(values, first, WINDOW, 0)
        up_rows = lax.dynamic_slice_in_dim(upstream, row, QBLOCK, 0)
        weights = jnp.where(allowed[None], jnp.exp(raw - logsum[number][..., None]), 0.0)
        d_weights = jnp.einsum("qhd,khd->hqk", up_rows, v_rows, preferred_element_type=jnp.float32)
        delta = jnp.sum(weights * d_weights, axis=-1, keepdims=True)
        d_scores = (weights * (d_weights - delta)).astype(jnp.bfloat16)
        d_query = (
            jnp.einsum("hqk,khd->qhd", d_scores, k_rows, preferred_element_type=jnp.float32) * scale
        )
        d_key = (
            jnp.einsum("hqk,qhd->khd", d_scores, q_rows, preferred_element_type=jnp.float32) * scale
        )
        d_value = jnp.einsum(
            "hqk,qhd->khd",
            weights.astype(jnp.bfloat16),
            up_rows,
            preferred_element_type=jnp.float32,
        )
        key_acc = lax.dynamic_update_slice_in_dim(
            key_acc, lax.dynamic_slice_in_dim(key_acc, first, WINDOW, 0) + d_key, first, 0
        )
        value_acc = lax.dynamic_update_slice_in_dim(
            value_acc, lax.dynamic_slice_in_dim(value_acc, first, WINDOW, 0) + d_value, first, 0
        )
        return ((key_acc, value_acc), d_query.astype(jnp.bfloat16))

    zeros = jnp.zeros(queries.shape, jnp.float32)
    (key_acc, value_acc), d_query = lax.scan(
        one_block, (zeros, zeros), jnp.arange(blocks, dtype=jnp.int32)
    )
    return (
        d_query.reshape(queries.shape),
        key_acc.astype(jnp.bfloat16),
        value_acc.astype(jnp.bfloat16),
    )


def local(
    tokens,
    lengths,
    attention_gain,
    query_weight,
    key_weight,
    value_weight,
    output_weight,
    feedforward_gain,
    gate_weight,
    up_weight,
    down_weight,
    cotangent,
):
    rows = tokens.shape[0]
    parts = lax.axis_size("seq")
    rank = lax.axis_index("seq")
    group = rows * parts
    per_device = HEADS // parts
    share = HEADS // KV_HEADS
    segment, position = layout(lengths[0], group)
    own_position = lax.dynamic_slice_in_dim(position, rank * rows, rows, 0)
    cos_t, sin_t = angles(own_position)
    head_ids = rank * per_device + jnp.arange(per_device, dtype=jnp.int32)
    key_ids = head_ids // share
    gain_one, w_query, w_key, w_value, w_output = (
        lax.all_gather(attention_gain, "seq", axis=0, tiled=True),
        lax.all_gather(query_weight, "seq", axis=0, tiled=True),
        lax.all_gather(key_weight, "seq", axis=0, tiled=True),
        lax.all_gather(value_weight, "seq", axis=0, tiled=True),
        lax.all_gather(output_weight, "seq", axis=0, tiled=True),
    )
    inputs = tokens.astype(jnp.float32)
    scale_one = lax.rsqrt(jnp.mean(inputs * inputs, axis=1, keepdims=True) + EPS)
    gain_a = gain_one.astype(jnp.float32)
    normed = (inputs * scale_one * gain_a).astype(jnp.bfloat16)
    q_proj = dot_plain(normed, w_query).reshape(rows, HEADS, HEAD_DIM)
    k_proj = dot_plain(normed, w_key).reshape(rows, KV_HEADS, HEAD_DIM)
    v_proj = dot_plain(normed, w_value).reshape(rows, KV_HEADS, HEAD_DIM)
    queries = rotate(q_proj, cos_t, sin_t, 1.0).astype(jnp.bfloat16)
    keys = rotate(k_proj, cos_t, sin_t, 1.0).astype(jnp.bfloat16)
    values = v_proj.astype(jnp.bfloat16)
    q_heads = lax.all_to_all(queries, "seq", split_axis=1, concat_axis=0, tiled=True)
    k_every, v_every = (
        lax.all_gather(keys, "seq", axis=0, tiled=True),
        lax.all_gather(values, "seq", axis=0, tiled=True),
    )
    k_heads = jnp.take(k_every, key_ids, axis=1)
    v_heads = jnp.take(v_every, key_ids, axis=1)
    mixed_heads, logsum = attend(q_heads, k_heads, v_heads, segment, position)
    mixed = lax.all_to_all(mixed_heads, "seq", split_axis=0, concat_axis=1, tiled=True).reshape(
        rows, D
    )
    middle = inputs + dot_plain(mixed, w_output)
    scale_two = lax.rsqrt(jnp.mean(middle * middle, axis=1, keepdims=True) + EPS)
    gain_two, w_gate, w_up, w_down = (
        lax.all_gather(feedforward_gain, "seq", axis=0, tiled=True),
        lax.all_gather(gate_weight, "seq", axis=0, tiled=True),
        lax.all_gather(up_weight, "seq", axis=0, tiled=True),
        lax.all_gather(down_weight, "seq", axis=0, tiled=True),
    )
    gain_f = gain_two.astype(jnp.float32)
    normed_two = (middle * scale_two * gain_f).astype(jnp.bfloat16)
    gate = dot_plain(normed_two, w_gate)
    up_part = dot_plain(normed_two, w_up)
    sigma = jax.nn.sigmoid(gate)
    hidden = (gate * sigma * up_part).astype(jnp.bfloat16)
    layer_output = (middle + dot_plain(hidden, w_down)).astype(jnp.bfloat16)
    gain_two, w_gate, w_up, w_down = (
        lax.all_gather(feedforward_gain, "seq", axis=0, tiled=True),
        lax.all_gather(gate_weight, "seq", axis=0, tiled=True),
        lax.all_gather(up_weight, "seq", axis=0, tiled=True),
        lax.all_gather(down_weight, "seq", axis=0, tiled=True),
    )
    down_grad = dot_left(hidden, cotangent)
    d_hidden = dot_right(cotangent, w_down)
    d_up = (d_hidden * gate * sigma).astype(jnp.bfloat16)
    d_gate = (d_hidden * up_part * sigma * (1.0 + gate * (1.0 - sigma))).astype(jnp.bfloat16)
    gate_grad = dot_left(normed_two, d_gate)
    up_grad = dot_left(normed_two, d_up)
    d_normed_two = dot_right(d_gate, w_gate) + dot_right(d_up, w_up)
    gain_f_grad = jnp.sum(d_normed_two * middle * scale_two, axis=0)
    d_middle = cotangent.astype(jnp.float32) + norm_back(d_normed_two * gain_f, middle, scale_two)
    gain_f_part, gate_part, up_piece, down_part = (
        lax.psum_scatter(
            gain_f_grad.astype(jnp.bfloat16), "seq", scatter_dimension=0, tiled=True
        ).astype(jnp.float32),
        lax.psum_scatter(
            gate_grad.astype(jnp.bfloat16), "seq", scatter_dimension=0, tiled=True
        ).astype(jnp.float32),
        lax.psum_scatter(
            up_grad.astype(jnp.bfloat16), "seq", scatter_dimension=0, tiled=True
        ).astype(jnp.float32),
        lax.psum_scatter(
            down_grad.astype(jnp.bfloat16), "seq", scatter_dimension=0, tiled=True
        ).astype(jnp.float32),
    )
    gain_one, w_query, w_key, w_value, w_output = (
        lax.all_gather(attention_gain, "seq", axis=0, tiled=True),
        lax.all_gather(query_weight, "seq", axis=0, tiled=True),
        lax.all_gather(key_weight, "seq", axis=0, tiled=True),
        lax.all_gather(value_weight, "seq", axis=0, tiled=True),
        lax.all_gather(output_weight, "seq", axis=0, tiled=True),
    )
    d_attention = d_middle.astype(jnp.bfloat16)
    output_grad = dot_left(mixed, d_attention)
    d_mixed = dot_right(d_attention, w_output).astype(jnp.bfloat16).reshape(rows, HEADS, HEAD_DIM)
    d_heads = lax.all_to_all(d_mixed, "seq", split_axis=1, concat_axis=0, tiled=True)
    dq_heads, dk_heads, dv_heads = attend_back(
        q_heads, k_heads, v_heads, d_heads, logsum, segment, position
    )
    d_queries, key_copies, value_copies = (
        lax.all_to_all(dq_heads, "seq", split_axis=0, concat_axis=1, tiled=True),
        lax.all_to_all(dk_heads, "seq", split_axis=0, concat_axis=1, tiled=True),
        lax.all_to_all(dv_heads, "seq", split_axis=0, concat_axis=1, tiled=True),
    )
    d_keys = jnp.sum(
        key_copies.astype(jnp.float32).reshape(rows, KV_HEADS, share, HEAD_DIM), axis=2
    )
    d_values = jnp.sum(
        value_copies.astype(jnp.float32).reshape(rows, KV_HEADS, share, HEAD_DIM), axis=2
    )
    dq_proj = (
        rotate(d_queries.astype(jnp.float32), cos_t, sin_t, -1.0)
        .astype(jnp.bfloat16)
        .reshape(rows, D)
    )
    dk_proj = (
        rotate(d_keys, cos_t, sin_t, -1.0).astype(jnp.bfloat16).reshape(rows, KV_HEADS * HEAD_DIM)
    )
    dv_proj = d_values.astype(jnp.bfloat16).reshape(rows, KV_HEADS * HEAD_DIM)
    query_grad = dot_left(normed, dq_proj)
    key_grad = dot_left(normed, dk_proj)
    value_grad = dot_left(normed, dv_proj)
    d_normed = dot_right(dq_proj, w_query) + dot_right(dk_proj, w_key) + dot_right(dv_proj, w_value)
    gain_a_grad = jnp.sum(d_normed * inputs * scale_one, axis=0)
    token_gradient = d_middle + norm_back(d_normed * gain_a, inputs, scale_one)
    gain_a_part, query_part, key_part, value_part, output_part = (
        lax.psum_scatter(
            gain_a_grad.astype(jnp.bfloat16), "seq", scatter_dimension=0, tiled=True
        ).astype(jnp.float32),
        lax.psum_scatter(
            query_grad.astype(jnp.bfloat16), "seq", scatter_dimension=0, tiled=True
        ).astype(jnp.float32),
        lax.psum_scatter(
            key_grad.astype(jnp.bfloat16), "seq", scatter_dimension=0, tiled=True
        ).astype(jnp.float32),
        lax.psum_scatter(
            value_grad.astype(jnp.bfloat16), "seq", scatter_dimension=0, tiled=True
        ).astype(jnp.float32),
        lax.psum_scatter(
            output_grad.astype(jnp.bfloat16), "seq", scatter_dimension=0, tiled=True
        ).astype(jnp.float32),
    )
    summed = (
        lax.psum(gain_a_part.astype(jnp.bfloat16), "dp").astype(jnp.float32),
        lax.psum(query_part.astype(jnp.bfloat16), "dp").astype(jnp.float32),
        lax.psum(key_part.astype(jnp.bfloat16), "dp").astype(jnp.float32),
        lax.psum(value_part.astype(jnp.bfloat16), "dp").astype(jnp.float32),
        lax.psum(output_part.astype(jnp.bfloat16), "dp").astype(jnp.float32),
        lax.psum(gain_f_part.astype(jnp.bfloat16), "dp").astype(jnp.float32),
        lax.psum(gate_part.astype(jnp.bfloat16), "dp").astype(jnp.float32),
        lax.psum(up_piece.astype(jnp.bfloat16), "dp").astype(jnp.float32),
        lax.psum(down_part.astype(jnp.bfloat16), "dp").astype(jnp.float32),
    )
    return (
        layer_output,
        token_gradient,
        summed[0],
        summed[1],
        summed[2],
        summed[3],
        summed[4],
        summed[5],
        summed[6],
        summed[7],
        summed[8],
    )


def solution(mesh):
    return jax.shard_map(
        local,
        mesh=mesh,
        in_specs=(
            P(("dp", "seq"), None),
            P("dp", None),
            P("seq"),
            P("seq", None),
            P("seq", None),
            P("seq", None),
            P("seq", None),
            P("seq"),
            P("seq", None),
            P("seq", None),
            P("seq", None),
            P(("dp", "seq"), None),
        ),
        out_specs=(
            P(("dp", "seq"), None),
            P(("dp", "seq"), None),
            P("seq"),
            P("seq", None),
            P("seq", None),
            P("seq", None),
            P("seq", None),
            P("seq"),
            P("seq", None),
            P("seq", None),
            P("seq", None),
        ),
        check_vma=False,
    )
```

profile of v0, /device:TPU:28, one launch (start us, length us, event | category | flops | bytes accessed | tf_op | source)
XLA Modules:
  0.0 2695.1 jit_solution(17340416585490386061)
XLA Ops:
  34.8 19.7 all-gather.18.cloned.1.call-done
  59.5 77.3 %all-gather.12.cloned.1.call-done = bf16[2048,2048]{1,0:T(8,128)(2,1)} async-done(((bf16[256,2048]{1,0:T(8,128)(2,1)}), bf16[2048,2048]{1,0:T(8,128)(2,1)}) %all-gather.12.cloned.1.call-update) | async-done | bytes 8388624 | tf_op jit(solution)/shard_map/all_gather | solution.py:175
  153.8 38.0 %all-gather.16.cloned.1.call-done = bf16[2560,4,64]{2,1,0:T(4,128)(2,1)} async-done(((bf16[320,4,64]{2,1,0:T(4,128)(2,1)}), bf16[2560,4,64]{2,1,0:T(4,128)(2,1)}) %all-gather.16.cloned.1.call-update) | async-done | bytes 1310736 | tf_op jit(solution)/shard_map/all_gather | solution.py:192
  196.3 30.4 %all-gather.20.cloned.1.call-done = bf16[2560,4,64]{2,1,0:T(4,128)(2,1)} async-done(((bf16[320,4,64]{2,1,0:T(4,128)(2,1)}), bf16[2560,4,64]{2,1,0:T(4,128)(2,1)}) %all-gather.20.cloned.1.call-update) | async-done | bytes 1310736 | tf_op jit(solution)/shard_map/all_gather | solution.py:193
  243.6 129.8 %while.27 = (s32[]{:T(128)}, bf16[5,512,4,64]{1,3,2,0:T(8,128)(2,1)}, f32[5,4,512]{2,1,0:T(4,128)S(1)}, s32[5]{0:T(128)S(1)}, s32[2560]{0:T(1024)S(1)}, /*index=...) while((s32[]{:T(128)}, ...), condition=%wide.region_7.9_spmd, body=%wide.region_4.8_spmd.sunk | while | flops 1409153024 | bytes 155288304 | solution.py:98
  389.2 64.6 %all-gather.1 = bf16[8,1,256]{2,1,0:T(2,128)(2,1)S(1)} all-gather(bf16[1,1,256]{2,1,0:T(2,128)(2,1)S(1)} %reshape.326), channel_id=1, replica_groups=mesh['dp'=4,'seq'=8] {'seq'}, dimensions={0}, use_global_device_ids=true | all-gather | bytes 4608 | tf_op jit(solution)/shard_map/all_gather | solution.py:204
  469.9 69.5 %all-gather.24.cloned.1.call-done = bf16[2048,5632]{1,0:T(8,128)(2,1)} async-done(((bf16[256,5632]{1,0:T(8,128)(2,1)}), bf16[2048,5632]{1,0:T(8,128)(2,1)}) %all-gather.24.cloned.1.call-update) | async-done | bytes 23068688 | tf_op jit(solution)/shard_map/all_gather | solution.py:205
  539.4 15.9 fusion.64
  555.2 186.6 %all-gather.26.cloned.1.call-done = bf16[2048,5632]{1,0:T(8,128)(2,1)} async-done(((bf16[256,5632]{1,0:T(8,128)(2,1)}), bf16[2048,5632]{1,0:T(8,128)(2,1)}) %all-gather.26.cloned.1.call-update) | async-done | bytes 23068688 | tf_op jit(solution)/shard_map/all_gather | solution.py:206
  756.2 188.2 %all-gather.28.cloned.1.call-done = bf16[5632,2048]{1,0:T(8,128)(2,1)} async-done(((bf16[704,2048]{1,0:T(8,128)(2,1)}), bf16[5632,2048]{1,0:T(8,128)(2,1)}) %all-gather.28.cloned.1.call-update) | async-done | bytes 23068688 | tf_op jit(solution)/shard_map/all_gather | solution.py:207
  944.4 27.3 %multiply_convert_fusion.1 = (bf16[320,5632]{1,0:T(8,128)(2,1)}, bf16[320,5632]{1,0:T(8,128)(2,1)}, bf16[320,5632]{1,0:T(8,128)(2,1)}) fusion(f32[320,5632]{1,0:T(8,128)} %fusion.64, f32[320,5632]{1,0:T(8,128)} %fusion.65, bf16[320,2048]{1,0:T(8,128)(2,1)S(1)} %copy-done.19, bf16[5632,2048]{1,0:T(8,128)(2,1)} %all-gather.28.cloned.1.call-done), kind=kOutput, calls=%fused_computation.52 | convolution fusion | flops 7410810880 | bytes 49610752 | tf_op jit(solution)/shard_map/dot_general | solution.py:56
  986.1 16.3 multiply_reduce_fusion.1
  1022.7 35.3 %all-to-all-done.2 = bf16[320,32,64]{0,2,1:T(8,128)(2,1)} async-done(((bf16[320,32,64]{0,2,1:T(8,128)(2,1)}), bf16[320,32,64]{0,2,1:T(8,128)(2,1)}, u32[]{:S(2)}, u32[]{:S(2)}) %all-to-all-start.2) | async-done | bytes 1310752 | tf_op jit(solution)/shard_map/all_to_all | solution.py:255
  1066.3 374.0 %while.28 = (s32[]{:T(128)}, f32[2560,4,64]{0,2,1:T(8,128)}, f32[2560,4,64]{0,2,1:T(8,128)}, bf16[5,512,4,64]{1,3,2,0:T(8,128)(2,1)}, s32[5]{0:T(128)S(1)}, /*in...) while((s32[]{:T(128)}, f32[2560,4,64]{0,2,1:T(8,128)}, ...), condition=%wide.region_12.14_spmd.clone, body=%wide.region_10.13_spmd.clone.sunk | while | flops 3441555456 | bytes 236020624 | solution.py:138
  1096.7 19.2 multiply_convert_fusion.6
  1169.8 19.2 multiply_convert_fusion.6
  1229.4 15.5 multiply_reduce_fusion.5
  1244.9 19.2 multiply_convert_fusion.6
  1304.5 15.5 multiply_reduce_fusion.5
  1320.0 19.2 multiply_convert_fusion.6
  1395.1 19.2 multiply_convert_fusion.6
  1465.1 21.7 all-to-all-done.4
  1506.5 21.3 all-to-all-done.5
  1557.4 53.0 %all_to_all.78 = bf16[8,2,40960]{2,1,0:T(2,128)(2,1)} all-to-all(bf16[8,2,40960]{2,1,0:T(2,128)(2,1)S(1)} %reshape.338), channel_id=1, replica_groups=mesh['dp'=4,'seq'=8] {'seq'}, dimensions={0} | all-to-all | bytes 2621440 | tf_op jit(solution)/shard_map/all_to_all | solution.py:260
  1634.3 17.3 convolution_convert_fusion.2
  1651.6 17.3 convolution_convert_fusion.1
  1670.3 17.6 convolution_convert_fusion
  1688.1 76.8 %reduce-scatter.8.cloned.1.call-done = bf16[256,2048]{1,0:T(8,128)(2,1)} async-done(((bf16[2048,2048]{1,0:T(8,128)(2,1)}), bf16[256,2048]{1,0:T(8,128)(2,1)}) %reduce-scatter.8.cloned.1.call-update) | async-done | bytes 1048592 | tf_op jit(solution)/shard_map/reduce_scatter | solution.py:289
  1764.8 228.0 %reduce-scatter.16.cloned.1.call-done = bf16[256,5632]{1,0:T(8,128)(2,1)} async-done(((bf16[2048,5632]{1,0:T(8,128)(2,1)}), bf16[256,5632]{1,0:T(8,128)(2,1)}) %reduce-scatter.16.cloned.1.call-update) | async-done | bytes 2883600 | tf_op jit(solution)/shard_map/reduce_scatter | solution.py:235
  1992.9 228.0 %reduce-scatter.18.cloned.1.call-done = bf16[256,5632]{1,0:T(8,128)(2,1)} async-done(((bf16[2048,5632]{1,0:T(8,128)(2,1)}), bf16[256,5632]{1,0:T(8,128)(2,1)}) %reduce-scatter.18.cloned.1.call-update) | async-done | bytes 2883600 | tf_op jit(solution)/shard_map/reduce_scatter | solution.py:238
  2220.9 228.0 %reduce-scatter.20.cloned.1.call-done = bf16[704,2048]{1,0:T(8,128)(2,1)} async-done(((bf16[5632,2048]{1,0:T(8,128)(2,1)}), bf16[704,2048]{1,0:T(8,128)(2,1)}) %reduce-scatter.20.cloned.1.call-update) | async-done | bytes 2883600 | tf_op jit(solution)/shard_map/reduce_scatter | solution.py:241
  2504.3 167.5 %all-reduce.7.cloned.1.call-done = (bf16[256,2048]{1,0:T(8,128)(2,1)}, bf16[256,256]{1,0:T(8,128)(2,1)}, bf16[256,256]{1,0:T(8,128)(2,1)}, bf16[256,2048]{1,0:T(...) async-done(((bf16[256,2048]{1,0:T(8,128)(2,1)}, bf16[256,256]{1,0:T(8,128)(2,1)}, bf16[256,256]{1,0:T(8,128)(2,1)}, ...) | async-done | bytes 11010064 | tf_op jit(solution)/shard_map/psum | solution.py:304
  (372 shorter events, 689.5 us)
Async XLA Ops:
  7.2 24.0 all-gather.14.cloned.1.call-start
  7.9 46.5 %all-gather.18.cloned.1.call-start = ((), (), s32[]{:S(2)}) async-start(), calls=%async_computation.16 | async-start | bytes 1179648 | tf_op jit(solution)/shard_map/all_gather | solution.py:177
  8.7 128.1 %all-gather.12.cloned.1.call-start = ((), (), s32[]{:S(2)}) async-start(), calls=%async_computation.13 | async-start | bytes 9437184 | tf_op jit(solution)/shard_map/all_gather | solution.py:175
  9.4 182.4 %all-gather.16.cloned.1.call-start = ((), (), s32[]{:S(2)}) async-start(), calls=%async_computation.15 | async-start | bytes 2949120 | tf_op jit(solution)/shard_map/all_gather | solution.py:192
  18.7 118.0 %copy-start.36 = (f32[8,1,256]{2,1,0:T(1,128)}, f32[8,1,256]{2,1,0:T(1,128)S(1)}, u32[]{:S(2)}) copy-start(f32[8,1,256]{2,1,0:T(1,128)S(1)} %convert_element_type.241) | copy-start | bytes 24580
  21.4 115.4 %copy-start.38 = (f32[320]{0:T(512)}, f32[320]{0:T(512)S(1)}, u32[]{:S(2)}) copy-start(f32[320]{0:T(512)S(1)} %add_rsqrt_fusion.1) | copy-start | bytes 3844
  22.3 121.5 %copy-start.23 = (f32[320,32]{0,1:T(8,128)}, f32[320,32]{0,1:T(8,128)S(1)}, u32[]{:S(2)}) copy-start(f32[320,32]{0,1:T(8,128)S(1)} %get-tuple-element.244) | copy-start | bytes 122884
  34.7 192.0 %all-gather.20.cloned.1.call-start = ((), (), s32[]{:S(2)}) async-start(), calls=%async_computation.17 | async-start | bytes 2949120 | tf_op jit(solution)/shard_map/all_gather | solution.py:193
  57.4 404.7 %all-gather.22.cloned.1.call-start = ((), (), s32[]{:S(2)}) async-start(), calls=%async_computation.18 | async-start | bytes 9437184 | tf_op jit(solution)/shard_map/all_gather | solution.py:178
  58.0 481.4 %all-gather.24.cloned.1.call-start = ((), (), s32[]{:S(2)}) async-start(), calls=%async_computation.19 | async-start | bytes 25952256 | tf_op jit(solution)/shard_map/all_gather | solution.py:205
  58.7 683.1 %all-gather.26.cloned.1.call-start = ((), (), s32[]{:S(2)}) async-start(), calls=%async_computation.20 | async-start | bytes 25952256 | tf_op jit(solution)/shard_map/all_gather | solution.py:206
  145.8 89.3 %all-to-all-start = ((bf16[320,32,64]{0,2,1:T(8,128)(2,1)}), bf16[320,32,64]{0,2,1:T(8,128)(2,1)}, u32[]{:S(2)}, u32[]{:S(2)}) async-start(bf16[320,32,64]{0,2,1:T(8,128)(2,1)} %pad_maximum_fusion), calls=%async_computation | async-start | bytes 3145728 | tf_op jit(solution)/shard_map/all_to_all | solution.py:190
  153.0 791.4 %all-gather.28.cloned.1.call-start = ((), (), s32[]{:S(2)}) async-start(), calls=%async_computation.21 | async-start | bytes 25952256 | tf_op jit(solution)/shard_map/all_gather | solution.py:207
  382.8 71.0 %all-to-all-start.1 = ((bf16[8,2,40960]{2,1,0:T(2,128)(2,1)}), bf16[8,2,40960]{2,1,0:T(2,128)(2,1)S(1)}, u32[]{:S(2)}, u32[]{:S(2)}) async-start(bf16[8,2,40960]{2,1,0:T(2,128)(2,1)} %reshape.336), calls=%async_computation.1 | async-start | bytes 2621440 | tf_op jit(solution)/shard_map/all_to_all | solution.py:198
  469.9 69.5 %copy-start.21 = (bf16[320,2048]{1,0:T(8,128)(2,1)}, bf16[320,2048]{1,0:T(8,128)(2,1)S(1)}, u32[]{:S(2)}) copy-start(bf16[320,2048]{1,0:T(8,128)(2,1)S(1)} %multiply_convert_fusion.4) | copy-start | bytes 3932164
  555.2 389.2 %copy-start.19 = (bf16[320,2048]{1,0:T(8,128)(2,1)S(1)}, bf16[320,2048]{1,0:T(8,128)(2,1)}, u32[]{:S(2)}) copy-start(bf16[320,2048]{1,0:T(8,128)(2,1)} %param.29) | copy-start | bytes 3932164
  1015.2 42.8 %all-to-all-start.2 = ((bf16[320,32,64]{0,2,1:T(8,128)(2,1)}), bf16[320,32,64]{0,2,1:T(8,128)(2,1)}, u32[]{:S(2)}, u32[]{:S(2)}) async-start(bf16[320,32,64]{0,2,1:T(8,128)(2,1)} %bitcast.160), calls=%async_computation.2 | async-start | bytes 3145728 | tf_op jit(solution)/shard_map/all_to_all | solution.py:255
  1069.4 27.3 %copy-start.2 = (pred[512,2560]{1,0:T(8,128)(4,1)}, pred[512,2560]{1,0:T(8,128)(4,1)S(1)}, u32[]{:S(2)}) copy-start(pred[512,2560]{1,0:T(8,128)(4,1)S(1)} %compare_and_fusion.6) | copy-start | bytes 3932164 | tf_op jit(solution)/shard_map/while
  1142.5 27.3 %copy-start.2 = (pred[512,2560]{1,0:T(8,128)(4,1)}, pred[512,2560]{1,0:T(8,128)(4,1)S(1)}, u32[]{:S(2)}) copy-start(pred[512,2560]{1,0:T(8,128)(4,1)S(1)} %compare_and_fusion.6) | copy-start | bytes 3932164 | tf_op jit(solution)/shard_map/while
  1217.6 27.3 %copy-start.2 = (pred[512,2560]{1,0:T(8,128)(4,1)}, pred[512,2560]{1,0:T(8,128)(4,1)S(1)}, u32[]{:S(2)}) copy-start(pred[512,2560]{1,0:T(8,128)(4,1)S(1)} %compare_and_fusion.6) | copy-start | bytes 3932164 | tf_op jit(solution)/shard_map/while
  1292.7 27.3 %copy-start.2 = (pred[512,2560]{1,0:T(8,128)(4,1)}, pred[512,2560]{1,0:T(8,128)(4,1)S(1)}, u32[]{:S(2)}) copy-start(pred[512,2560]{1,0:T(8,128)(4,1)S(1)} %compare_and_fusion.6) | copy-start | bytes 3932164 | tf_op jit(solution)/shard_map/while
  1367.8 27.3 %copy-start.2 = (pred[512,2560]{1,0:T(8,128)(4,1)}, pred[512,2560]{1,0:T(8,128)(4,1)S(1)}, u32[]{:S(2)}) copy-start(pred[512,2560]{1,0:T(8,128)(4,1)S(1)} %compare_and_fusion.6) | copy-start | bytes 3932164 | tf_op jit(solution)/shard_map/while
  1450.1 36.7 %all-to-all-start.4 = ((bf16[8,2,40960]{2,1,0:T(2,128)(2,1)}), bf16[8,2,40960]{2,1,0:T(2,128)(2,1)}, u32[]{:S(2)}, u32[]{:S(2)}) async-start(bf16[8,2,40960]{2,1,0:T(2,128)(2,1)} %reshape.340), calls=%async_computation.4 | async-start | bytes 2621440 | tf_op jit(solution)/shard_map/all_to_all | solution.py:261
  1486.8 41.0 %all-to-all-start.5 = ((bf16[8,2,40960]{2,1,0:T(2,128)(2,1)}), bf16[8,2,40960]{2,1,0:T(2,128)(2,1)}, u32[]{:S(2)}, u32[]{:S(2)}) async-start(bf16[8,2,40960]{2,1,0:T(2,128)(2,1)} %reshape.342), calls=%async_computation.5 | async-start | bytes 2621440 | tf_op jit(solution)/shard_map/all_to_all | solution.py:262
  1493.6 194.4 %reduce-scatter.10.cloned.1.call-start = ((), (), s32[]{:S(2)}) async-start(), calls=%async_computation.23 | async-start | bytes 1179648 | tf_op jit(solution)/shard_map/reduce_scatter | solution.py:292
  1506.5 181.6 %reduce-scatter.12.cloned.1.call-start = ((), (), s32[]{:S(2)}) async-start(), calls=%async_computation.24 | async-start | bytes 1179648 | tf_op jit(solution)/shard_map/reduce_scatter | solution.py:295
  1540.4 147.7 %reduce-scatter.14.cloned.1.call-start = ((), (), s32[]{:S(2)}) async-start(), calls=%async_computation.25 | async-start | bytes 9437184 | tf_op jit(solution)/shard_map/reduce_scatter | solution.py:298
  1548.9 215.9 %reduce-scatter.8.cloned.1.call-start = ((), (), s32[]{:S(2)}) async-start(), calls=%async_computation.22 | async-start | bytes 9437184 | tf_op jit(solution)/shard_map/reduce_scatter | solution.py:289
  1632.9 359.9 %reduce-scatter.16.cloned.1.call-start = ((), (), s32[]{:S(2)}) async-start(), calls=%async_computation.26 | async-start | bytes 25952256 | tf_op jit(solution)/shard_map/reduce_scatter | solution.py:235
  1651.6 569.4 %reduce-scatter.18.cloned.1.call-start = ((), (), s32[]{:S(2)}) async-start(), calls=%async_computation.27 | async-start | bytes 25952256 | tf_op jit(solution)/shard_map/reduce_scatter | solution.py:238
  1669.0 780.0 %reduce-scatter.20.cloned.1.call-start = ((), (), s32[]{:S(2)}) async-start(), calls=%async_computation.28 | async-start | bytes 25952256 | tf_op jit(solution)/shard_map/reduce_scatter | solution.py:241
  1687.9 983.9 %all-reduce.7.cloned.1.call-start = ((), (), s32[]{:S(2)}) async-start(), calls=%async_computation.29 | async-start | bytes 22020096 | tf_op jit(solution)/shard_map/psum | solution.py:304
  (53 other events, 333.6 us)
Sparse Core Ops, SparseCore 0:
  9.6 21.5 all-gather.13
  32.8 21.6 all-gather.17
  56.1 80.6 all-gather.11
  138.8 52.8 all-gather.15
  193.8 32.8 all-gather.19
  228.2 80.4 all-gather.21
  310.3 228.9 all-gather.23
  541.0 200.7 all-gather.25
  743.5 200.8 all-gather.27
  1506.6 31.1 reduce-scatter.9
  1540.5 32.1 reduce-scatter.11
  1574.8 94.7 reduce-scatter.13
  1671.9 92.8 reduce-scatter.7
  1767.0 225.7 reduce-scatter.15
  1995.1 225.7 reduce-scatter.17
  2223.1 225.7 reduce-scatter.19
  2453.5 218.2 all-reduce.6
where the time goes:
time: 2710 us; the launch traced here: 2700 us
  waiting for transfers between devices  1630 us (60%)
  matrix products  542 us (20%)
  other arithmetic  181 us (7%)
  blocking collectives  148 us (5%)
  local copies, waits for them, and re-layouts  126 us (5%)
  starting transfers between devices  36 us (1%)
    reduce_scatter x1, waiting for transfers between devices, local(): lax.psum_scatter(gate_grad.astype(jnp.bfloat16), 'seq', scatter_dimension...  228 us
    reduce_scatter x1, waiting for transfers between devices, local(): lax.psum_scatter(down_grad.astype(jnp.bfloat16), 'seq', scatter_dimension...  228 us
    reduce_scatter x1, waiting for transfers between devices, local(): lax.psum_scatter(up_grad.astype(jnp.bfloat16), 'seq', scatter_dimension=0...  228 us
    all_gather x1, waiting for transfers between devices, local(): lax.all_gather(down_weight, 'seq', axis=0, tiled=True)  188 us
    all_gather x1, waiting for transfers between devices, local(): lax.all_gather(up_weight, 'seq', axis=0, tiled=True)  187 us
    psum x1, waiting for transfers between devices, local(): lax.psum(query_part.astype(jnp.bfloat16), 'dp').astype(jnp.float32)  168 us
    convert_element_type x5, other arithmetic, one_block(): d_scores = (weights * (d_weights - delta)).astype(jnp.bfloat16)  96.1 us
    dot_general x5, matrix products, one_block(): jnp.einsum('qhd,khd->hqk', up_rows, v_rows, preferred_element_type=jnp.fl...  77.4 us
  transfers between devices with their start and end apart: 22, of which 16 were waited for; matrix products, arithmetic and copies ran while one was open for 14% of the time, Pallas kernels for 0%

commit v1 on v0

v1 whole, which is shorter than its diff:
```python
import functools

import jax
import jax.numpy as jnp
from jax import lax
from jax.experimental import pallas as pl
from jax.experimental.pallas import tpu as pltpu
from jax.sharding import PartitionSpec as P

HEADS = 32
HEAD_DIM = 64
KV_HEADS = 4
EPS = 1e-05
ROPE_BASE = 10000.0
NEG = -1e30
VMEM_LIMIT = 56 * 2**20
BF = jnp.bfloat16
F32 = jnp.float32

NT = (((1,), (1,)), ((), ()))
TN = (((0,), (0,)), ((), ()))
NN = (((1,), (0,)), ((), ()))


def dot(left, right, dims=NN):
    return lax.dot_general(left, right, dims, preferred_element_type=F32)


def params(*semantics):
    return pltpu.CompilerParams(
        dimension_semantics=semantics, vmem_limit_bytes=VMEM_LIMIT
    )


def pick_kernel(which, gain, gate, up, out, *, shards):
    piece = gate.shape[1] // (4 * shards)
    for quarter in range(4):

        @pl.when(which[0] == quarter)
        def _():
            scale = gain[...]
            parts = []
            for source in (gate, up):
                whole = source[...].astype(F32) * scale
                for shard in range(shards):
                    first = (shard * 4 + quarter) * piece
                    parts.append(whole[:, first : first + piece])
            out[...] = jnp.concatenate(parts, axis=1).astype(BF)


def pick_columns(quarter, gain, gate, up, shards):
    rows, width = gate.shape
    return pl.pallas_call(
        functools.partial(pick_kernel, shards=shards),
        out_shape=jax.ShapeDtypeStruct((rows, width // 2), BF),
        in_specs=[
            pl.BlockSpec(memory_space=pltpu.SMEM),
            pl.BlockSpec(memory_space=pltpu.VMEM),
            pl.BlockSpec(memory_space=pltpu.VMEM),
            pl.BlockSpec(memory_space=pltpu.VMEM),
        ],
        out_specs=pl.BlockSpec(memory_space=pltpu.VMEM),
        compiler_params=params(),
        name="pick_columns",
    )(quarter, gain, gate, up)


def spread_kernel(grads, gain, gate, up, gate_out, up_out, gain_out, *, shards):
    half = grads.shape[2] // 2
    piece = half // shards
    total = 0.0
    for source, out, first in ((gate, gate_out, 0), (up, up_out, half)):
        parts = []
        for shard in range(shards):
            for quarter in range(4):
                begin = first + shard * piece
                parts.append(grads[quarter, :, begin : begin + piece].astype(F32))
        whole = jnp.concatenate(parts, axis=1)
        total = total + jnp.sum(
            whole * source[...].astype(F32), axis=1, keepdims=True
        )
        out[...] = whole * gain[...]
    gain_out[...] = total


def spread_columns(grads, gain, gate, up, shards):
    rows, width = gate.shape
    block = min(rows, 64)
    row = lambda cols: pl.BlockSpec((block, cols), lambda i: (i, 0))
    return pl.pallas_call(
        functools.partial(spread_kernel, shards=shards),
        grid=(rows // block,),
        out_shape=(
            jax.ShapeDtypeStruct((rows, width), F32),
            jax.ShapeDtypeStruct((rows, width), F32),
            jax.ShapeDtypeStruct((rows, 1), F32),
        ),
        in_specs=[
            pl.BlockSpec((4, block, width // 2), lambda i: (0, i, 0)),
            row(1),
            row(width),
            row(width),
        ],
        out_specs=(row(width), row(width), row(1)),
        compiler_params=params("arbitrary"),
        name="spread_columns",
    )(grads, gain, gate, up)


def turn(values, cos_t, sin_t):
    lane = lax.broadcasted_iota(jnp.int32, values.shape, 1)
    other = jnp.where(
        lane % 64 < 32, pltpu.roll(values, 96, 1), pltpu.roll(values, 32, 1)
    )
    return values * cos_t + other * sin_t


def project_kernel(x_ref, w_ref, cos_ref, sin_ref, hat_ref, q_ref, kv_ref):
    x = x_ref[...].astype(F32)
    scale = lax.rsqrt(jnp.mean(x * x, axis=1, keepdims=True) + EPS)
    hat = (x * scale).astype(BF)
    hat_ref[...] = hat
    out = dot(hat, w_ref[...])
    cos_t, sin_t = cos_ref[...], sin_ref[...]
    wide = q_ref.shape[1]
    for pair in range(wide // 128):
        part = turn(out[:, pair * 128 : pair * 128 + 128], cos_t, sin_t)
        q_ref[:, pair * 128 : pair * 128 + 128] = (part * HEAD_DIM**-0.5).astype(BF)
    kv = out[:, wide : wide + 128]
    lane = lax.broadcasted_iota(jnp.int32, kv.shape, 1)
    kv_ref[...] = jnp.where(lane < 64, turn(kv, cos_t, sin_t), kv).astype(BF)


def project(x, weight, cos_t, sin_t, rows):
    count, depth = x.shape
    wide = weight.shape[1] - 128
    row = lambda cols: pl.BlockSpec((rows, cols), lambda i: (i, 0))
    return pl.pallas_call(
        project_kernel,
        grid=(count // rows,),
        out_shape=(
            jax.ShapeDtypeStruct((count, depth), BF),
            jax.ShapeDtypeStruct((count, wide), BF),
            jax.ShapeDtypeStruct((count, 128), BF),
        ),
        in_specs=[
            row(depth),
            pl.BlockSpec(weight.shape, lambda i: (0, 0)),
            row(128),
            row(128),
        ],
        out_specs=(row(depth), row(wide), row(128)),
        compiler_params=params("arbitrary"),
        name="project",
    )(x, weight, cos_t, sin_t)


def stack_heads(source, target, rows, upper):
    lane = lax.broadcasted_iota(jnp.int32, (rows, 128), 1)
    keep = (lane >= 64) if upper else (lane < 64)
    for head in range(source.shape[1] // 64):
        slab = source[:, head // 2 * 128 : head // 2 * 128 + 128].astype(F32)
        if (head % 2 == 1) != upper:
            slab = pltpu.roll(slab, 64, 1)
        target[head * rows : head * rows + rows, :] = jnp.where(keep, slab, 0.0).astype(BF)


def allowed(bounds, chunk, rows):
    low = bounds[0:1, :] - chunk * rows
    high = bounds[1:2, :] - chunk * rows
    place = lax.broadcasted_iota(jnp.int32, (rows, bounds.shape[1]), 0)
    return (place >= low) & (place <= high)


def attend_kernel(where, q_ref, kv_ref, bound_ref, out_ref, lse_ref, stacked, *, rows):
    group = pl.program_id(0)
    first, last = where[group], where[4]
    stack_heads(q_ref, stacked, rows, False)
    bounds = bound_ref[0]
    lane = lax.broadcasted_iota(jnp.int32, (rows, 128), 1)
    for pair in range(q_ref.shape[1] // 128):
        queries = stacked[pair * 2 * rows : (pair + 1) * 2 * rows, :]

        def step(chunk, carry):
            top, total, acc = carry
            kv = kv_ref[chunk]
            scores = jnp.where(allowed(bounds, chunk, rows), dot(kv, queries, NT), NEG)
            peak = jnp.maximum(top, jnp.max(scores, axis=0, keepdims=True))
            fade = jnp.exp(top - peak)
            weights = jnp.exp(scores - peak)
            total = total * fade + jnp.sum(weights, axis=0, keepdims=True)
            acc = acc * fade + dot(kv, weights.astype(BF), TN)
            return peak, total, acc

        start = (
            jnp.full((1, 2 * rows), NEG, F32),
            jnp.zeros((1, 2 * rows), F32),
            jnp.zeros((128, 2 * rows), F32),
        )
        top, total, acc = lax.fori_loop(first, last + 1, step, start)
        lse_ref[0, pair : pair + 1, :] = top + jnp.log(total)
        flat = (acc / total).T
        out_ref[:, pair * 128 : pair * 128 + 128] = jnp.where(
            lane < 64, pltpu.roll(flat[:rows], 64, 1), flat[rows:]
        ).astype(BF)


def attend(where, queries, kv, bounds, rows):
    shards = kv.shape[0]
    wide = queries.shape[1]
    pairs = wide // 128
    return pl.pallas_call(
        functools.partial(attend_kernel, rows=rows),
        grid_spec=pltpu.PrefetchScalarGridSpec(
            num_scalar_prefetch=1,
            grid=(4,),
            in_specs=[
                pl.BlockSpec((rows, wide), lambda g, w: (g, 0)),
                pl.BlockSpec((shards, rows, 128), lambda g, w: (0, g, 0)),
                pl.BlockSpec((1, 2, 2 * rows), lambda g, w: (g, 0, 0)),
            ],
            out_specs=(
                pl.BlockSpec((rows, wide), lambda g, w: (g, 0)),
                pl.BlockSpec((1, pairs, 2 * rows), lambda g, w: (g, 0, 0)),
            ),
            scratch_shapes=[pltpu.VMEM((2 * pairs * rows, 128), BF)],
        ),
        out_shape=(
            jax.ShapeDtypeStruct((4 * rows, wide), BF),
            jax.ShapeDtypeStruct((4, pairs, 2 * rows), F32),
        ),
        compiler_params=params("arbitrary"),
        name="attend",
    )(where, queries, kv, bounds)


def attend_back_kernel(
    where,
    q_ref,
    kv_ref,
    bound_ref,
    up_ref,
    out_ref,
    lse_ref,
    cos_ref,
    sin_ref,
    dq_ref,
    dkv_ref,
    stacked,
    upward,
    dq_acc,
    *,
    rows,
):
    group = pl.program_id(0)
    first, last = where[group], where[4]
    shards = kv_ref.shape[0]
    pairs = q_ref.shape[1] // 128
    stack_heads(q_ref, stacked, rows, False)
    stack_heads(up_ref, upward, rows, True)
    bounds = bound_ref[0]
    lane = lax.broadcasted_iota(jnp.int32, (rows, 128), 1)
    deltas = []
    for pair in range(pairs):
        slab = up_ref[:, pair * 128 : pair * 128 + 128].astype(F32)
        slab = slab * out_ref[:, pair * 128 : pair * 128 + 128].astype(F32)
        both = jnp.concatenate(
            [jnp.where(lane < 64, slab, 0.0), jnp.where(lane < 64, 0.0, slab)], axis=0
        )
        deltas.append(jnp.sum(both.T, axis=0, keepdims=True))
        dq_acc[pair] = jnp.zeros((128, 2 * rows), F32)

    def clear(chunk, carry):
        dkv_ref[chunk] = jnp.zeros((rows, 128), BF)
        return carry

    lax.fori_loop(0, first, clear, 0)
    lax.fori_loop(last + 1, shards, clear, 0)

    def step(chunk, carry):
        kv = kv_ref[chunk]
        mask = allowed(bounds, chunk, rows)
        total = jnp.zeros((rows, 128), F32)
        for pair in range(pairs):
            queries = stacked[pair * 2 * rows : (pair + 1) * 2 * rows, :]
            ups = upward[pair * 2 * rows : (pair + 1) * 2 * rows, :]
            scores = dot(kv, queries, NT)
            weights = jnp.where(
                mask, jnp.exp(scores - lse_ref[0, pair : pair + 1, :]), 0.0
            )
            d_scores = (weights * (dot(kv, ups, NT) - deltas[pair])).astype(BF)
            total = total + dot(d_scores, queries) + dot(weights.astype(BF), ups)
            dq_acc[pair] += dot(kv, d_scores, TN)
        dkv_ref[chunk] = total.astype(BF)
        return carry

    lax.fori_loop(first, last + 1, step, 0)
    cos_t, sin_t = cos_ref[...], sin_ref[...]
    for pair in range(pairs):
        flat = dq_acc[pair].T
        slab = jnp.where(lane < 64, flat[:rows], pltpu.roll(flat[rows:], 64, 1))
        dq_ref[:, pair * 128 : pair * 128 + 128] = turn(
            slab * HEAD_DIM**-0.5, cos_t, -sin_t
        ).astype(BF)


def attend_back(where, queries, kv, bounds, upstream, out, lse, cos_t, sin_t, rows):
    shards = kv.shape[0]
    wide = queries.shape[1]
    pairs = wide // 128
    row = lambda cols: pl.BlockSpec((rows, cols), lambda g, w: (g, 0))
    every = pl.BlockSpec((shards, rows, 128), lambda g, w: (0, g, 0))
    return pl.pallas_call(
        functools.partial(attend_back_kernel, rows=rows),
        grid_spec=pltpu.PrefetchScalarGridSpec(
            num_scalar_prefetch=1,
            grid=(4,),
            in_specs=[
                row(wide),
                every,
                pl.BlockSpec((1, 2, 2 * rows), lambda g, w: (g, 0, 0)),
                row(wide),
                row(wide),
                pl.BlockSpec((1, pairs, 2 * rows), lambda g, w: (g, 0, 0)),
                row(128),
                row(128),
            ],
            out_specs=(row(wide), every),
            scratch_shapes=[
                pltpu.VMEM((2 * pairs * rows, 128), BF),
                pltpu.VMEM((2 * pairs * rows, 128), BF),
                pltpu.VMEM((pairs, 128, 2 * rows), F32),
            ],
        ),
        out_shape=(
            jax.ShapeDtypeStruct((4 * rows, wide), BF),
            jax.ShapeDtypeStruct(kv.shape, BF),
        ),
        compiler_params=params("arbitrary"),
        name="attend_back",
    )(where, queries, kv, bounds, upstream, out, lse, cos_t, sin_t)


def hop(value, step):
    return lax.ppermute(value, "dp", [(i, i ^ step) for i in range(4)])


def gather_plane(value):
    half = value.shape[0] // 2
    one = hop(value, 1)
    two = hop(value, 2)
    three = jnp.concatenate([hop(two[:half], 1), hop(one[half:], 2)], axis=0)
    return [value, one, two, three]


def reduce_plane(parts):
    own, one, two, three = parts
    half = own.shape[0] // 2
    by_one = hop(three[:half], 1)
    by_two = hop(three[half:], 2)
    add = lambda a, b: (a.astype(F32) + b.astype(F32)).astype(BF)
    two = jnp.concatenate([add(two[:half], by_one), two[half:]], axis=0)
    one = jnp.concatenate([one[:half], add(one[half:], by_two)], axis=0)
    return own.astype(F32) + hop(one, 1).astype(F32) + hop(two, 2).astype(F32)


def heads_to_tokens(value, rows):
    mine = lax.axis_index("dp")
    parts = [value[:rows]] + [
        hop(value[k * rows : (k + 1) * rows], k) for k in range(1, 4)
    ]
    return in_order(parts, mine, 1)


def in_order(parts, mine, axis):
    one = mine % 2 == 1
    two = mine // 2 == 1
    low = [jnp.where(one, parts[1], parts[0]), jnp.where(one, parts[0], parts[1])]
    high = [jnp.where(one, parts[3], parts[2]), jnp.where(one, parts[2], parts[3])]
    first = [jnp.where(two, b, a) for a, b in zip(low, high, strict=True)]
    second = [jnp.where(two, a, b) for a, b in zip(low, high, strict=True)]
    return jnp.concatenate(first + second, axis=axis)


def tokens_to_heads(value):
    mine = lax.axis_index("dp")
    wide = value.shape[1] // 4
    parts = [
        lax.dynamic_slice_in_dim(value, (mine ^ k) * wide, wide, 1) for k in range(4)
    ]
    return jnp.concatenate(
        [parts[0]] + [hop(parts[k], k) for k in range(1, 4)], axis=0
    )


def local(
    tokens,
    lengths,
    attention_gain,
    query_weight,
    key_weight,
    value_weight,
    output_weight,
    feedforward_gain,
    gate_weight,
    up_weight,
    down_weight,
    cotangent,
):
    rows, depth = tokens.shape
    shards = lax.axis_size("seq")
    mine = lax.axis_index("dp")
    place = lax.axis_index("seq")
    wide = HEADS // KV_HEADS * HEAD_DIM
    near = lambda v: lax.all_gather(v, "seq", axis=0, tiled=True)
    far = lambda v: lax.psum_scatter(v, "seq", scatter_dimension=0, tiled=True)

    gain_a = attention_gain.astype(F32)[:, None]
    gain_f = feedforward_gain.astype(F32)[:, None]
    own_qkv = jnp.concatenate(
        [
            lax.dynamic_slice_in_dim(query_weight, mine * wide, wide, 1),
            lax.dynamic_slice_in_dim(key_weight, mine * HEAD_DIM, HEAD_DIM, 1),
            lax.dynamic_slice_in_dim(value_weight, mine * HEAD_DIM, HEAD_DIM, 1),
        ],
        axis=1,
    )
    w_qkv = near((own_qkv.astype(F32) * gain_a).astype(BF))
    w_out = near(output_weight)
    w_gu = near(pick_columns(mine[None], gain_f, gate_weight, up_weight, shards))
    piece = down_weight.shape[0] // 4
    w_down = near(lax.dynamic_slice_in_dim(down_weight, mine * piece, piece, 0))

    every = lax.all_gather(lengths, "dp", axis=0, tiled=True)
    order = mine ^ jnp.arange(4, dtype=jnp.int32)
    chosen = order[:, None] == jnp.arange(4, dtype=jnp.int32)[None, :]
    sizes = jnp.sum(jnp.where(chosen[:, :, None], every[None], 0), axis=1)
    count = sizes.shape[1]
    before = jnp.arange(count)[:, None] <= jnp.arange(count)[None, :]
    ends = jnp.sum(jnp.where(before[None], sizes[:, :, None], 0), axis=1)
    index = place * rows + jnp.arange(rows, dtype=jnp.int32)
    passed = ends[:, None, :] <= index[None, :, None]
    begin = jnp.max(jnp.where(passed, ends[:, None, :], 0), axis=2)
    position = (index[None, :] - begin).astype(F32).reshape(4 * rows)
    half = HEAD_DIM // 2
    inverse = ROPE_BASE ** (-jnp.arange(half, dtype=F32) * 2.0 / HEAD_DIM)
    theta = position[:, None] * inverse[None, :]
    cos_h, sin_h = jnp.cos(theta), jnp.sin(theta)
    cos_t = jnp.concatenate([cos_h] * 4, axis=1)
    sin_t = jnp.concatenate([-sin_h, sin_h] * 2, axis=1)
    bounds = jnp.stack(
        [begin, jnp.broadcast_to(index[None, :], begin.shape)], axis=1
    )
    bounds = jnp.concatenate([bounds, bounds], axis=2)
    where = jnp.concatenate([begin[:, 0] // rows, place[None]])

    x = jnp.concatenate(gather_plane(tokens), axis=0)
    hat, queries, own_kv = project(x, w_qkv, cos_t, sin_t, rows)
    kv = lax.all_gather(own_kv, "seq", axis=0)
    mixed_heads, lse = attend(where, queries, kv, bounds, rows)
    mixed = heads_to_tokens(mixed_heads, rows)
    middle = tokens.astype(F32) + dot(mixed, w_out)
    scale_two = lax.rsqrt(jnp.mean(middle * middle, axis=1, keepdims=True) + EPS)
    hat_two = (middle * scale_two).astype(BF)

    hats = gather_plane(hat_two)
    dys = gather_plane(cotangent)
    columns = w_gu.shape[1] // 2
    hiddens, d_gus, outs, d_hats = [], [], [], []
    for hat_k, dy_k in zip(hats, dys, strict=True):
        both = dot(hat_k, w_gu)
        gate, up = both[:, :columns], both[:, columns:]
        d_hidden = dot(dy_k, w_down, NT)
        sigma = jax.nn.sigmoid(gate)
        silu = gate * sigma
        hidden = (silu * up).astype(BF)
        d_gate = d_hidden * up * (sigma + silu * (1.0 - sigma))
        d_gu = jnp.concatenate(
            [d_gate.astype(BF), (d_hidden * silu).astype(BF)], axis=1
        )
        hiddens.append(hidden)
        d_gus.append(d_gu)
        d_hats.append(dot(d_gu, w_gu, NT).astype(BF))
    for hidden in hiddens:
        outs.append(dot(hidden, w_down).astype(BF))
    e = reduce_plane(d_hats)
    layer_output = (middle + reduce_plane(outs)).astype(BF)
    hidden_all = jnp.concatenate(hiddens, axis=0)
    d_gu_all = jnp.concatenate(d_gus, axis=0)
    down_part = far(dot(hidden_all, jnp.concatenate(dys, axis=0), TN).astype(BF))
    gu_part = far(dot(jnp.concatenate(hats, axis=0), d_gu_all, TN).astype(BF))

    inner = jnp.mean(e * middle, axis=1, keepdims=True)
    d_middle = (
        cotangent.astype(F32)
        + scale_two * e
        - middle * (scale_two * scale_two * scale_two * inner)
    )
    d_attention = d_middle.astype(BF)

    d_mixed = dot(d_attention, w_out, NT).astype(BF)
    d_heads = tokens_to_heads(d_mixed)
    out_part = far(dot(mixed, d_attention, TN).astype(BF))
    dq, dkv = attend_back(
        where, queries, kv, bounds, d_heads, mixed_heads, lse, cos_t, sin_t, rows
    )
    own_dkv = far(dkv.reshape(shards * 4 * rows, 128)).astype(F32)
    first, second = own_dkv[:, :half], own_dkv[:, half : 2 * half]
    d_qkv = jnp.concatenate(
        [
            dq,
            (first * cos_h + second * sin_h).astype(BF),
            (second * cos_h - first * sin_h).astype(BF),
            own_dkv[:, HEAD_DIM:].astype(BF),
        ],
        axis=1,
    )
    f = reduce_plane(
        [
            dot(d_qkv[k * rows : (k + 1) * rows], w_qkv, NT).astype(BF)
            for k in range(4)
        ]
    )
    qkv_part = far(dot(hat, d_qkv, TN).astype(BF))
    inputs = tokens.astype(F32)
    scale_one = lax.rsqrt(jnp.mean(inputs * inputs, axis=1, keepdims=True) + EPS)
    inner = jnp.mean(f * inputs, axis=1, keepdims=True)
    token_gradient = (
        d_middle
        + scale_one * f
        - inputs * (scale_one * scale_one * scale_one * inner)
    )

    gu_all = lax.all_gather(gu_part, "dp", axis=0)
    gate_gradient, up_gradient, gain_f_gradient = spread_columns(
        gu_all, gain_f, gate_weight, up_weight, shards
    )
    down_gradient = lax.all_gather(down_part, "dp", axis=0, tiled=True).astype(F32)
    output_gradient = lax.psum(out_part, "dp").astype(F32)
    qkv_all = lax.all_gather(qkv_part, "dp", axis=0).astype(F32)
    join = lambda a, b: jnp.concatenate([qkv_all[k, :, a:b] for k in range(4)], axis=1)
    raw_q = join(0, wide)
    raw_k = join(wide, wide + HEAD_DIM)
    raw_v = join(wide + HEAD_DIM, wide + 2 * HEAD_DIM)
    gain_a_gradient = (
        jnp.sum(raw_q * query_weight.astype(F32), axis=1)
        + jnp.sum(raw_k * key_weight.astype(F32), axis=1)
        + jnp.sum(raw_v * value_weight.astype(F32), axis=1)
    )
    return (
        layer_output,
        token_gradient,
        gain_a_gradient,
        raw_q * gain_a,
        raw_k * gain_a,
        raw_v * gain_a,
        output_gradient,
        gain_f_gradient[:, 0],
        gate_gradient,
        up_gradient,
        down_gradient,
    )


def solution(mesh):
    both = P(("dp", "seq"), None)
    flat = P("seq")
    split = P("seq", None)
    return jax.shard_map(
        local,
        mesh=mesh,
        in_specs=(
            both,
            P("dp", None),
            flat,
            split,
            split,
            split,
            split,
            flat,
            split,
            split,
            split,
            both,
        ),
        out_specs=(
            both,
            both,
            flat,
            split,
            split,
            split,
            split,
            flat,
            split,
            split,
            split,
        ),
        check_vma=False,
    )
```

time: 2710 us -> 1220 us (0.45)
  waiting for transfers between devices: 1630 us -> 730 us
  matrix products: 542 us -> 171 us
  other arithmetic: 181 us -> 46.8 us
  Pallas kernels: 0 us -> 133 us
  blocking collectives: 148 us -> 32.1 us
  local copies, waits for them, and re-layouts: 126 us -> 53.4 us
    reduce_scatter x7 -> x5, waiting for transfers between devices: 761 us -> 300 us  [local(): far = lambda v: lax.psum_scatter(v, 'seq', scatter_dimension=0, tiled=True)]
    all_gather x9 -> x8, waiting for transfers between devices: 619 us -> 190 us  [the longest x4 89.5 us: local(): near = lambda v: lax.all_gather(v, 'seq', axis=0, tiled=True)]
    dot_general x56 -> x26, matrix products: 542 us -> 171 us  [dot(): return lax.dot_general(left, right, dims, preferred_element_type=F32)]
    ppermute x0 -> x30, waiting for transfers between devices: none -> 187 us  [hop(): return lax.ppermute(value, 'dp', [(i, i ^ step) for i in range(4)])]
    pallas_call x0 -> x5, Pallas kernels: none -> 133 us  [the longest x1 53.7 us: attend(): pl.pallas_call(functools.partial(attend_kernel, rows=rows), grid_spec=plt...]
    psum x1, waiting for transfers between devices: 168 us -> 50.5 us  [local(): output_gradient = lax.psum(out_part, 'dp').astype(F32)]
    convert_element_type x20 -> x14, other arithmetic: 118 us -> 19.9 us  [the longest x1 5.12 us: local(): lax.all_gather(down_part, 'dp', axis=0, tiled=True).astype(F32)]
    all_to_all x5 -> x0, waiting for transfers between devices: 78.4 us -> none  [the longest x1 35.3 us: local(): lax.all_to_all(d_mixed, 'seq', split_axis=1, concat_axis=0, tiled=True)]
  transfers between devices with their start and end apart: 22 -> 44, of which waited for: 16 -> 28; matrix products, arithmetic and copies ran while one was open for 14% -> 17% of each run, Pallas kernels for 0% -> 5%
where the time goes in v1:
time: 1220 us; the launch traced here: 1210 us
  waiting for transfers between devices  730 us (60%)
  matrix products  171 us (14%)
  Pallas kernels  133 us (11%)
  local copies, waits for them, and re-layouts  53.4 us (4%)
  other arithmetic  46.8 us (4%)
  starting transfers between devices  32.9 us (3%)
  blocking collectives  32.1 us (3%)
  between operations  15.4 us (1%)
    reduce_scatter x5, waiting for transfers between devices, local(): far = lambda v: lax.psum_scatter(v, 'seq', scatter_dimension=0, tiled=True)  300 us
    ppermute x30, waiting for transfers between devices, hop(): return lax.ppermute(value, 'dp', [(i, i ^ step) for i in range(4)])  187 us
    dot_general x26, matrix products, dot(): return lax.dot_general(left, right, dims, preferred_element_type=F32)  171 us
    all_gather x4, waiting for transfers between devices, local(): near = lambda v: lax.all_gather(v, 'seq', axis=0, tiled=True)  89.5 us
    all_gather x1, waiting for transfers between devices, local(): gu_all = lax.all_gather(gu_part, 'dp', axis=0)  64.8 us
    pallas_call x1, Pallas kernels, attend(): pl.pallas_call(functools.partial(attend_kernel, rows=rows), grid_spec=plt...  53.7 us
    pallas_call x1, Pallas kernels, attend_back(): pl.pallas_call(functools.partial(attend_back_kernel, rows=rows), grid_spe...  53.6 us
    psum x1, waiting for transfers between devices, local(): output_gradient = lax.psum(out_part, 'dp').astype(F32)  50.5 us
  transfers between devices with their start and end apart: 44, of which 28 were waited for; matrix products, arithmetic and copies ran while one was open for 17% of the time, Pallas kernels for 5%

profile of v1, /device:TPU:28, one launch (start us, length us, event | category | flops | bytes accessed | tf_op | source)
XLA Modules:
  0.0 1214.2 jit_solution(10935056450304502487)
XLA Ops:
  13.0 32.1 %all-gather.3 = s32[4,1,2]{2,1,0:T(1,128)S(1)} all-gather(s32[1,1,2]{2,1,0:T(1,128)} %bitcast.83), channel_id=1, replica_groups=mesh['dp'=4,'seq'=8] {'dp'}, dimensions={0}, use_global_device_ids=true | all-gather | bytes 40 | tf_op jit(solution)/shard_map/all_gather | solution.py:434
  71.0 10.2 project.1
  90.5 23.1 %all-gather.23.cloned.1.call-done = bf16[10240,128]{1,0:T(8,128)(2,1)} async-done(((bf16[1280,128]{1,0:T(8,128)(2,1)}), bf16[10240,128]{1,0:T(8,128)(2,1)}) %all-gather.23.cloned.1.call-update) | async-done | bytes 2621456 | tf_op jit(solution)/shard_map/all_gather | solution.py:459
  113.6 53.7 %attend.1 = (bf16[1280,512]{1,0:T(8,128)(2,1)}, f32[4,4,640]{2,1,0:T(4,128)}) custom-call(s32[5]{0:T(128)} %pad_add_fusion.where, bf16[1280,512]{1,0:T(8,128)(2,1)} %get-tuple-element.21.q_ref, bf16[8,1280,128]{2,1,0:T(8,128)(2,1)} %bitcast.76, s32[4,2,640]{2,1,0:T(2,128)} %add_add_fusion.bound_ref), custom_call_target="tpu_custom_call" | custom-call | tf_op jit(solution)/shard_map/attend/pallas_call | solution.py:212
  182.2 13.5 %all-gather.15.cloned.1.call-done = bf16[2048,2048]{1,0:T(8,128)(2,1)} async-done(((bf16[256,2048]{1,0:T(8,128)(2,1)}), bf16[2048,2048]{1,0:T(8,128)(2,1)}) %all-gather.15.cloned.1.call-update) | async-done | bytes 8388624 | tf_op jit(solution)/shard_map/all_gather | solution.py:415
  208.1 27.6 %collective-permute-done.7 = bf16[320,2048]{1,0:T(8,128)(2,1)S(1)} collective-permute-done((bf16[320,2048]{1,0:T(8,128)(2,1)S(1)}, bf16[320,2048]{1,0:T(8,128)(2,1)S(1)}, u32[]{:S(2)}, u32[]{:S(2)}) %collective-permute-start.7) | collective-permute-done | bytes 1310752 | tf_op jit(solution)/shard_map/ppermute | solution.py:345
  241.6 22.3 %collective-permute-done.15 = bf16[320,2048]{1,0:T(8,128)(2,1)} collective-permute-done((bf16[320,2048]{1,0:T(8,128)(2,1)}, bf16[320,2048]{1,0:T(8,128)(2,1)}, u32[]{:S(2)}, u32[]{:S(2)}) %collective-permute-start.15) | collective-permute-done | bytes 1310752 | tf_op jit(solution)/shard_map/ppermute | solution.py:345
  269.8 9.4 collective-permute-done.10
  279.3 25.0 %all-gather.17.cloned.1.call-done = bf16[2048,2816]{1,0:T(8,128)(2,1)} async-done(((bf16[256,2816]{1,0:T(8,128)(2,1)}), bf16[2048,2816]{1,0:T(8,128)(2,1)}) %all-gather.17.cloned.1.call-update) | async-done | bytes 11534352 | tf_op jit(solution)/shard_map/all_gather | solution.py:415
  304.2 10.2 fusion.42
  314.4 51.0 %all-gather.19.cloned.1.call-done = bf16[1408,2048]{1,0:T(8,128)(2,1)} async-done(((bf16[176,2048]{1,0:T(8,128)(2,1)}), bf16[1408,2048]{1,0:T(8,128)(2,1)}) %all-gather.19.cloned.1.call-update) | async-done | bytes 5767184 | tf_op jit(solution)/shard_map/all_gather | solution.py:415
  374.1 8.6 convolution_convert_fusion.14
  382.7 8.9 fusion.79
  430.1 8.9 convolution_convert_fusion.13
  439.0 8.7 convolution_convert_fusion.15
  466.9 22.4 %collective-permute-done.22 = bf16[320,2048]{1,0:T(8,128)(2,1)S(1)} collective-permute-done((bf16[320,2048]{1,0:T(8,128)(2,1)S(1)}, bf16[320,2048]{1,0:T(8,128)(2,1)S(1)}, u32[]{:S(2)}, u32[]{:S(2)}) %collective-permute-start.22) | collective-permute-done | bytes 1310752 | tf_op jit(solution)/shard_map/ppermute | solution.py:345
  492.1 9.7 multiply_reduce_fusion
  501.9 13.6 %collective-permute-done.14 = bf16[320,2048]{1,0:T(8,128)(2,1)S(1)} collective-permute-done((bf16[320,2048]{1,0:T(8,128)(2,1)}, bf16[320,2048]{1,0:T(8,128)(2,1)S(1)}, u32[]{:S(2)}, u32[]{:S(2)}) %collective-permute-start.14) | collective-permute-done | bytes 1310752 | tf_op jit(solution)/shard_map/ppermute | solution.py:345
  546.8 53.6 %attend_back.1 = (bf16[1280,512]{1,0:T(8,128)(2,1)}, bf16[8,1280,128]{2,1,0:T(8,128)(2,1)}) custom-call(s32[5]{0:T(128)} %pad_add_fusion.where, bf16[1280,512]{1,0:T(8,128)(2,1)} %get-tuple-element.21.q_ref, bf16[8,1280,128]{2,1,0:T(8,128)(2,1)} %bitcast.77, s32[4,2,640]{2,1,0:T(2,128)} %add_add_fusion.bound_ref, ...), custom_call_target="tpu_custom_call" | custom-call | tf_op jit(solution)/shard_map/attend_back/pallas_call | solution.py:313
  600.5 48.0 %reduce-scatter.6.cloned.1.call-done = bf16[1280,128]{1,0:T(8,128)(2,1)} async-done(((bf16[10240,128]{1,0:T(8,128)(2,1)}), bf16[1280,128]{1,0:T(8,128)(2,1)}) %reduce-scatter.6.cloned.1.call-update) | async-done | bytes 327696 | tf_op jit(solution)/shard_map/reduce_scatter | solution.py:416
  654.5 8.9 convolution_convert_fusion.3
  670.4 9.7 convolution_convert_fusion.1
  696.7 28.3 %convolution_convert_fusion = bf16[2048,2816]{1,0:T(8,128)(2,1)} fusion(bf16[1280,2048]{1,0:T(8,128)(2,1)} %constant_dynamic-update-slice_fusion.5, bf16[320,1408]{1,0:T(8,128)(2,1)} %get-tuple-element.40, bf16[320,1408]{1,0:T(8,128)(2,1)} %copy-done.46, bf16[320,1408]{1,0:T(8,128)(2,1)} %get-tuple-element.42, bf16[320,1408]{1,0:T(8,128)(2,1)} %get-tuple-element.41, ...), kind=kOutput, calls=%fused_computation | convolution fusion | flops 14827388928 | bytes 23986176 | tf_op jit(solution)/shard_map/dot_general | solution.py:26
  725.8 42.5 %reduce-scatter.14.cloned.1.call-done = bf16[176,2048]{1,0:T(8,128)(2,1)} async-done(((bf16[1408,2048]{1,0:T(8,128)(2,1)}), bf16[176,2048]{1,0:T(8,128)(2,1)}) %reduce-scatter.14.cloned.1.call-update) | async-done | bytes 720912 | tf_op jit(solution)/shard_map/reduce_scatter | solution.py:416
  768.4 90.2 %reduce-scatter.10.cloned.1.call-done = bf16[256,2048]{1,0:T(8,128)(2,1)} async-done(((bf16[2048,2048]{1,0:T(8,128)(2,1)}), bf16[256,2048]{1,0:T(8,128)(2,1)}) %reduce-scatter.10.cloned.1.call-update) | async-done | bytes 1048592 | tf_op jit(solution)/shard_map/reduce_scatter | solution.py:416
  859.0 119.5 %reduce-scatter.12.cloned.1.call-done = bf16[256,2816]{1,0:T(8,128)(2,1)} async-done(((bf16[2048,2816]{1,0:T(8,128)(2,1)}), bf16[256,2816]{1,0:T(8,128)(2,1)}) %reduce-scatter.12.cloned.1.call-update) | async-done | bytes 1441808 | tf_op jit(solution)/shard_map/reduce_scatter | solution.py:416
  986.6 15.2 %collective-permute-done.28 = bf16[160,2048]{1,0:T(8,128)(2,1)S(1)} collective-permute-done((bf16[160,2048]{1,0:T(8,128)(2,1)S(1)}, bf16[160,2048]{1,0:T(8,128)(2,1)S(1)}, u32[]{:S(2)}, u32[]{:S(2)}) %collective-permute-start.28) | collective-permute-done | bytes 655392 | tf_op jit(solution)/shard_map/ppermute | solution.py:345
  1007.5 40.0 %collective-permute-done.29 = bf16[320,2048]{1,0:T(8,128)(2,1)S(1)} collective-permute-done((bf16[320,2048]{1,0:T(8,128)(2,1)S(1)}, bf16[320,2048]{1,0:T(8,128)(2,1)S(1)}, u32[]{:S(2)}, u32[]{:S(2)}) %collective-permute-start.29) | collective-permute-done | bytes 1310752 | tf_op jit(solution)/shard_map/ppermute | solution.py:345
  1058.8 12.9 %all-gather.21.cloned.1.call-done = bf16[704,2048]{1,0:T(8,128)(2,1)} async-done(((bf16[176,2048]{1,0:T(8,128)(2,1)}), bf16[704,2048]{1,0:T(8,128)(2,1)}) %all-gather.21.cloned.1.call-update) | async-done | bytes 2883600 | tf_op jit(solution)/shard_map/all_gather | solution.py:538
  1076.8 50.5 %all-reduce.2.cloned.1.call-done = bf16[256,2048]{1,0:T(8,128)(2,1)} async-done(((bf16[256,2048]{1,0:T(8,128)(2,1)}), bf16[256,2048]{1,0:T(8,128)(2,1)}) %all-reduce.2.cloned.1.call-update) | async-done | bytes 1048592 | tf_op jit(solution)/shard_map/psum | solution.py:539
  1130.1 64.8 %all-gather.27.cloned.1.call-done = bf16[1024,2816]{1,0:T(8,128)(2,1)} async-done(((bf16[256,2816]{1,0:T(8,128)(2,1)}), bf16[1024,2816]{1,0:T(8,128)(2,1)}) %all-gather.27.cloned.1.call-update) | async-done | bytes 5767184 | tf_op jit(solution)/shard_map/all_gather | solution.py:534
  1194.9 10.7 spread_columns.1
  (303 shorter events, 245.2 us)
Async XLA Ops:
  7.2 63.8 %all-gather.13.cloned.1.call-start = ((), (), s32[]{:S(2)}) async-start(), calls=%async_computation.5 | async-start | bytes 2949120 | tf_op jit(solution)/shard_map/all_gather | solution.py:415
  10.9 102.7 %all-gather.23.cloned.1.call-start = ((), (), s32[]{:S(2)}) async-start(), calls=%async_computation.16 | async-start | bytes 2949120 | tf_op jit(solution)/shard_map/all_gather | solution.py:459
  11.0 43.8 %collective-permute-start = (bf16[320,2048]{1,0:T(8,128)(2,1)}, bf16[320,2048]{1,0:T(8,128)(2,1)}, u32[]{:S(2)}, u32[]{:S(2)}) collective-permute-start(bf16[320,2048]{1,0:T(8,128)(2,1)} %param.12), channel_id=1, source_target_pairs={{0,8},{8,0},{16,24},{24,16},{1,9},{9,1},{17,25},{25,17},{2,10},{10... | collective-permute-start | bytes 3932168 | tf_op jit(solution)/shard_map/ppermute | solution.py:345
  12.5 38.4 %collective-permute-start.1 = (bf16[320,2048]{1,0:T(8,128)(2,1)}, bf16[320,2048]{1,0:T(8,128)(2,1)}, u32[]{:S(2)}, u32[]{:S(2)}) collective-permute-start(bf16[320,2048]{1,0:T(8,128)(2,1)} %param.12), channel_id=1, source_target_pairs={{0,16},{8,24},{16,0},{24,8},{1,17},{9,25},{17,1},{25,9},{2,18},{10... | collective-permute-start | bytes 3932168 | tf_op jit(solution)/shard_map/ppermute | solution.py:345
  81.3 114.5 %all-gather.15.cloned.1.call-start = ((), (), s32[]{:S(2)}) async-start(), calls=%async_computation.6 | async-start | bytes 9437184 | tf_op jit(solution)/shard_map/all_gather | solution.py:415
  82.0 222.2 %all-gather.17.cloned.1.call-start = ((), (), s32[]{:S(2)}) async-start(), calls=%async_computation.7 | async-start | bytes 12976128 | tf_op jit(solution)/shard_map/all_gather | solution.py:415
  87.6 277.8 %all-gather.19.cloned.1.call-start = ((), (), s32[]{:S(2)}) async-start(), calls=%async_computation.8 | async-start | bytes 6488064 | tf_op jit(solution)/shard_map/all_gather | solution.py:415
  88.7 559.9 %reduce-scatter.6.cloned.1.call-start = ((), (), s32[]{:S(2)}) async-start(), calls=%async_computation.9 | async-start | bytes 2949120 | tf_op jit(solution)/shard_map/reduce_scatter | solution.py:416
  205.5 32.4 %collective-permute-start.8 = (bf16[320,2048]{1,0:T(8,128)(2,1)S(1)}, bf16[320,2048]{1,0:T(8,128)(2,1)S(1)}, u32[]{:S(2)}, u32[]{:S(2)}) collective-permute-start(bf16[320,2048]{1,0:T(8,128)(2,1)S(1)} %get-tuple-element.34), channel_id=1, source_target_pairs={{0,16},{8,24},{16,0},{24,8},{1,17},{9,25},{17,1},{25,9},{2,18},{10... | collective-permute-start | bytes 3932168 | tf_op jit(solution)/shard_map/ppermute | solution.py:345
  206.0 57.8 %collective-permute-start.15 = (bf16[320,2048]{1,0:T(8,128)(2,1)}, bf16[320,2048]{1,0:T(8,128)(2,1)}, u32[]{:S(2)}, u32[]{:S(2)}) collective-permute-start(bf16[320,2048]{1,0:T(8,128)(2,1)} %param.23), channel_id=1, source_target_pairs={{0,8},{8,0},{16,24},{24,16},{1,9},{9,1},{17,25},{25,17},{2,10},{10... | collective-permute-start | bytes 3932168 | tf_op jit(solution)/shard_map/ppermute | solution.py:345
  206.3 59.8 %collective-permute-start.16 = (bf16[320,2048]{1,0:T(8,128)(2,1)}, bf16[320,2048]{1,0:T(8,128)(2,1)}, u32[]{:S(2)}, u32[]{:S(2)}) collective-permute-start(bf16[320,2048]{1,0:T(8,128)(2,1)} %param.23), channel_id=1, source_target_pairs={{0,16},{8,24},{16,0},{24,8},{1,17},{9,25},{17,1},{25,9},{2,18},{10... | collective-permute-start | bytes 3932168 | tf_op jit(solution)/shard_map/ppermute | solution.py:345
  237.6 41.7 %collective-permute-start.10 = (bf16[160,2048]{1,0:T(8,128)(2,1)}, bf16[160,2048]{1,0:T(8,128)(2,1)S(1)}, u32[]{:S(2)}, u32[]{:S(2)}) collective-permute-start(bf16[160,2048]{1,0:T(8,128)(2,1)} %slice.235), channel_id=1, source_target_pairs={{0,16},{8,24},{16,0},{24,8},{1,17},{9,25},{17,1},{25,9},{2,18},{10... | collective-permute-start | bytes 1966088 | tf_op jit(solution)/shard_map/ppermute | solution.py:345
  239.8 39.4 %collective-permute-start.9 = (bf16[160,2048]{1,0:T(8,128)(2,1)}, bf16[160,2048]{1,0:T(8,128)(2,1)}, u32[]{:S(2)}, u32[]{:S(2)}) collective-permute-start(bf16[160,2048]{1,0:T(8,128)(2,1)} %slice.234), channel_id=1, source_target_pairs={{0,8},{8,0},{16,24},{24,16},{1,9},{9,1},{17,25},{25,17},{2,10},{10... | collective-permute-start | bytes 1966088 | tf_op jit(solution)/shard_map/ppermute | solution.py:345
  265.8 48.6 %collective-permute-start.18 = (bf16[160,2048]{1,0:T(8,128)(2,1)}, bf16[160,2048]{1,0:T(8,128)(2,1)}, u32[]{:S(2)}, u32[]{:S(2)}) collective-permute-start(bf16[160,2048]{1,0:T(8,128)(2,1)} %slice.247), channel_id=1, source_target_pairs={{0,16},{8,24},{16,0},{24,8},{1,17},{9,25},{17,1},{25,9},{2,18},{10... | collective-permute-start | bytes 1966088 | tf_op jit(solution)/shard_map/ppermute | solution.py:345
  268.1 46.3 %collective-permute-start.17 = (bf16[160,2048]{1,0:T(8,128)(2,1)}, bf16[160,2048]{1,0:T(8,128)(2,1)}, u32[]{:S(2)}, u32[]{:S(2)}) collective-permute-start(bf16[160,2048]{1,0:T(8,128)(2,1)} %slice.246), channel_id=1, source_target_pairs={{0,8},{8,0},{16,24},{24,16},{1,9},{9,1},{17,25},{25,17},{2,10},{10... | collective-permute-start | bytes 1966088 | tf_op jit(solution)/shard_map/ppermute | solution.py:345
  391.6 64.5 %collective-permute-start.21 = (bf16[160,2048]{1,0:T(8,128)(2,1)S(1)}, bf16[160,2048]{1,0:T(8,128)(2,1)}, u32[]{:S(2)}, u32[]{:S(2)}) collective-permute-start(bf16[160,2048]{1,0:T(8,128)(2,1)S(1)} %get-tuple-element.74), channel_id=1, source_target_pairs={{0,8},{8,0},{16,24},{24,16},{1,9},{9,1},{17,25},{25,17},{2,10},{10... | collective-permute-start | bytes 1966088 | tf_op jit(solution)/shard_map/ppermute | solution.py:345
  393.1 64.8 %collective-permute-start.19 = (bf16[160,2048]{1,0:T(8,128)(2,1)S(1)}, bf16[160,2048]{1,0:T(8,128)(2,1)}, u32[]{:S(2)}, u32[]{:S(2)}) collective-permute-start(bf16[160,2048]{1,0:T(8,128)(2,1)S(1)} %get-tuple-element.73), channel_id=1, source_target_pairs={{0,16},{8,24},{16,0},{24,8},{1,17},{9,25},{17,1},{25,9},{2,18},{10... | collective-permute-start | bytes 1966088 | tf_op jit(solution)/shard_map/ppermute | solution.py:345
  396.9 64.2 %collective-permute-start.13 = (bf16[160,2048]{1,0:T(8,128)(2,1)S(1)}, bf16[160,2048]{1,0:T(8,128)(2,1)S(1)}, u32[]{:S(2)}, u32[]{:S(2)}) collective-permute-start(bf16[160,2048]{1,0:T(8,128)(2,1)S(1)} %get-tuple-element.76), channel_id=1, source_target_pairs={{0,8},{8,0},{16,24},{24,16},{1,9},{9,1},{17,25},{25,17},{2,10},{10... | collective-permute-start | bytes 1966088 | tf_op jit(solution)/shard_map/ppermute | solution.py:345
  397.2 66.7 %collective-permute-start.11 = (bf16[160,2048]{1,0:T(8,128)(2,1)}, bf16[160,2048]{1,0:T(8,128)(2,1)}, u32[]{:S(2)}, u32[]{:S(2)}) collective-permute-start(bf16[160,2048]{1,0:T(8,128)(2,1)} %get-tuple-element.75), channel_id=1, source_target_pairs={{0,16},{8,24},{16,0},{24,8},{1,17},{9,25},{17,1},{25,9},{2,18},{10... | collective-permute-start | bytes 1966088 | tf_op jit(solution)/shard_map/ppermute | solution.py:345
  457.5 31.8 %collective-permute-start.22 = (bf16[320,2048]{1,0:T(8,128)(2,1)S(1)}, bf16[320,2048]{1,0:T(8,128)(2,1)S(1)}, u32[]{:S(2)}, u32[]{:S(2)}) collective-permute-start(bf16[320,2048]{1,0:T(8,128)(2,1)S(1)} %pad_maximum_fusion.6), channel_id=1, source_target_pairs={{0,16},{8,24},{16,0},{24,8},{1,17},{9,25},{17,1},{25,9},{2,18},{10... | collective-permute-start | bytes 3932168 | tf_op jit(solution)/shard_map/ppermute | solution.py:345
  462.4 53.0 %collective-permute-start.14 = (bf16[320,2048]{1,0:T(8,128)(2,1)}, bf16[320,2048]{1,0:T(8,128)(2,1)S(1)}, u32[]{:S(2)}, u32[]{:S(2)}) collective-permute-start(bf16[320,2048]{1,0:T(8,128)(2,1)} %pad_maximum_fusion.4), channel_id=1, source_target_pairs={{0,16},{8,24},{16,0},{24,8},{1,17},{9,25},{17,1},{25,9},{2,18},{10... | collective-permute-start | bytes 3932168 | tf_op jit(solution)/shard_map/ppermute | solution.py:345
  466.3 51.2 %collective-permute-start.12 = (bf16[320,2048]{1,0:T(8,128)(2,1)}, bf16[320,2048]{1,0:T(8,128)(2,1)}, u32[]{:S(2)}, u32[]{:S(2)}) collective-permute-start(bf16[320,2048]{1,0:T(8,128)(2,1)} %pad_maximum_fusion.3), channel_id=1, source_target_pairs={{0,8},{8,0},{16,24},{24,16},{1,9},{9,1},{17,25},{25,17},{2,10},{10... | collective-permute-start | bytes 3932168 | tf_op jit(solution)/shard_map/ppermute | solution.py:345
  600.5 124.6 %reduce-scatter.8.cloned.1.call-start = ((), (), s32[]{:S(2)}) async-start(), calls=%async_computation.10 | async-start | bytes 2949120 | tf_op jit(solution)/shard_map/reduce_scatter | solution.py:416
  663.4 104.9 %reduce-scatter.14.cloned.1.call-start = ((), (), s32[]{:S(2)}) async-start(), calls=%async_computation.14 | async-start | bytes 6488064 | tf_op jit(solution)/shard_map/reduce_scatter | solution.py:416
  680.1 178.5 %reduce-scatter.10.cloned.1.call-start = ((), (), s32[]{:S(2)}) async-start(), calls=%async_computation.11 | async-start | bytes 9437184 | tf_op jit(solution)/shard_map/reduce_scatter | solution.py:416
  689.9 288.5 %reduce-scatter.12.cloned.1.call-start = ((), (), s32[]{:S(2)}) async-start(), calls=%async_computation.13 | async-start | bytes 12976128 | tf_op jit(solution)/shard_map/reduce_scatter | solution.py:416
  725.1 328.1 %all-gather.25.cloned.1.call-start = ((), (), s32[]{:S(2)}) async-start(), calls=%async_computation.17 | async-start | bytes 1638400 | tf_op jit(solution)/shard_map/all_gather | solution.py:540
  725.8 345.9 %all-gather.21.cloned.1.call-start = ((), (), s32[]{:S(2)}) async-start(), calls=%async_computation.15 | async-start | bytes 3604480 | tf_op jit(solution)/shard_map/all_gather | solution.py:538
  768.3 359.0 %all-reduce.2.cloned.1.call-start = ((), (), s32[]{:S(2)}) async-start(), calls=%async_computation.12 | async-start | bytes 2097152 | tf_op jit(solution)/shard_map/psum | solution.py:539
  858.6 336.3 %all-gather.27.cloned.1.call-start = ((), (), s32[]{:S(2)}) async-start(), calls=%async_computation.18 | async-start | bytes 7208960 | tf_op jit(solution)/shard_map/all_gather | solution.py:534
  1002.2 45.3 %collective-permute-start.29 = (bf16[320,2048]{1,0:T(8,128)(2,1)S(1)}, bf16[320,2048]{1,0:T(8,128)(2,1)S(1)}, u32[]{:S(2)}, u32[]{:S(2)}) collective-permute-start(bf16[320,2048]{1,0:T(8,128)(2,1)S(1)} %pad_maximum_fusion.9), channel_id=1, source_target_pairs={{0,16},{8,24},{16,0},{24,8},{1,17},{9,25},{17,1},{25,9},{2,18},{10... | collective-permute-start | bytes 3932168 | tf_op jit(solution)/shard_map/ppermute | solution.py:345
  1006.0 43.2 %collective-permute-start.27 = (bf16[320,2048]{1,0:T(8,128)(2,1)S(1)}, bf16[320,2048]{1,0:T(8,128)(2,1)S(1)}, u32[]{:S(2)}, u32[]{:S(2)}) collective-permute-start(bf16[320,2048]{1,0:T(8,128)(2,1)S(1)} %pad_maximum_fusion.8), channel_id=1, source_target_pairs={{0,8},{8,0},{16,24},{24,16},{1,9},{9,1},{17,25},{25,17},{2,10},{10... | collective-permute-start | bytes 3932168 | tf_op jit(solution)/shard_map/ppermute | solution.py:345
  (66 other events, 815.9 us)
Sparse Core Ops, SparseCore 0:
  11.0 32.8 all-gather.12
  81.4 32.1 all-gather.22
  115.2 80.4 all-gather.14
  197.8 106.3 all-gather.16
  306.3 59.0 all-gather.18
  600.6 47.8 reduce-scatter.5
  663.6 36.5 reduce-scatter.7
  703.1 65.2 reduce-scatter.13
  770.6 87.9 reduce-scatter.9
  860.7 117.6 reduce-scatter.11
  980.3 39.5 all-gather.24
  1021.6 50.0 all-gather.20
  1074.8 52.4 all-reduce.1
  1129.0 65.8 all-gather.26
